TPU v7x, 256 devices: a whole 4x4x8 slice. The times are simulated.
256 devices in a mesh: var: 32 (over z_lo, x, core), tp: 8 (over z_hi, y).
Axes of the slice: x: 4, y: 4, z: 8 (z_hi: 2, z_lo: 4; z = z_hi * 4 + z_lo), core: 2. Of those that a mesh axis runs over, the one named last changes fastest.
Arguments:
- parent_inputs: bfloat16 [4096, 256], P('var'), may hold values from -6 to 6
- gate_parent: bfloat16 [4096, 7168], P('var', 'tp'), may hold values from -0.09375 to 0.09375
- up_parent: bfloat16 [4096, 7168], P('var', 'tp'), may hold values from -0.09375 to 0.09375
- down_parent: bfloat16 [7168, 4096], P('tp', 'var'), may hold values from -0.0625 to 0.0625
- targets: bfloat16 [256, 4096], P('var', 'tp'), may hold values from -6 to 6
- widths: int32 [32], P('var'), may hold values from 1792 to 7168, as said below
- gains: float32 [32, 7168], P('var', 'tp'), may hold values from 0.25 to 2
Outputs:
- down_grad: bfloat16 [32, 7168, 4096], P('var', 'tp')
- gain_grad: float32 [32, 7168], P('var', 'tp')
Inputs may be any that keep to these rules, and one draw needn't show every extreme that they name: `widths`: every draw has a variant of exactly 7168 and one of exactly 1792 kept hidden units.
All inputs are finite; a program needn't handle non-finite values.
Results may differ from a plain program's by a relative error of at most 0.0059.
Values may be sent and summed in bfloat16 or wider, within the bound.
No kernel may reach another device: no remote copies, remote signals or barrier semaphores. Data moves between devices by JAX's collectives and lax.ppermute only.
A program may use at most 128 MiB of HBM per device.

v0:
```python
import jax
import jax.numpy as jnp
from jax import lax
from jax.sharding import PartitionSpec as P


def local(parent_inputs, gate_parent, up_parent, down_parent, targets, widths, gains):
    contract_rows = (((0,), (0,)), ((), ()))
    rows = parent_inputs.shape[1]
    local_ff = gate_parent.shape[1]
    feats = lax.all_gather(parent_inputs, "var", axis=0, tiled=True)
    gate_piece = lax.all_gather(gate_parent, "var", axis=0, tiled=True)
    up_piece = lax.all_gather(up_parent, "var", axis=0, tiled=True)
    gate_sum = lax.dot_general(feats, gate_piece, contract_rows, preferred_element_type=jnp.float32)
    up_sum = lax.dot_general(feats, up_piece, contract_rows, preferred_element_type=jnp.float32)
    raw = jax.nn.silu(gate_sum) * up_sum
    column = lax.axis_index("tp") * local_ff + lax.broadcasted_iota(jnp.int32, (1, local_ff), 1)
    kept = (column < widths[0]).astype(jnp.float32)
    hidden = (raw * gains * kept).astype(jnp.bfloat16)
    down_whole = lax.all_gather(down_parent, "var", axis=1, tiled=True)
    partial_value = jnp.dot(hidden, down_whole, preferred_element_type=jnp.float32)
    target_part = lax.all_gather(targets, "var", axis=0, tiled=True)
    output = lax.psum(partial_value, "tp")
    target_whole = lax.all_gather(target_part, "tp", axis=1, tiled=True)
    residual = (output - target_whole.astype(jnp.float32)).astype(jnp.bfloat16)
    scale = 1.0 / rows**0.5
    grad_down = lax.dot_general(hidden, residual, contract_rows, preferred_element_type=jnp.float32)
    grad_down = (grad_down * scale).astype(jnp.bfloat16)[None]
    back = lax.dot_general(
        residual, down_whole, (((1,), (1,)), ((), ())), preferred_element_type=jnp.float32
    )
    grad_gain = kept * jnp.sum(raw * back, axis=0, keepdims=True) * scale
    return (grad_down, grad_gain)


def solution(mesh):
    return jax.shard_map(
        local,
        mesh=mesh,
        in_specs=(
            P("var", None),
            P("var", "tp"),
            P("var", "tp"),
            P("tp", "var"),
            P("var", "tp"),
            P("var"),
            P("var", "tp"),
        ),
        out_specs=(P("var", "tp", None), P("var", "tp")),
        check_vma=False,
    )
```

profile of v0, /device:TPU:1, one launch (start us, length us, event | category | flops | bytes accessed | tf_op | source)
XLA Modules:
  0.0 589.8 jit_solution(13577693330374438191)
XLA Ops:
  7.2 0.0 all-gather.6.cloned.1.call-start
  7.2 0.7 all-gather.6.cloned.1.call-update
  7.9 0.0 all-gather.8.cloned.1.call-start
  7.9 0.7 all-gather.8.cloned.1.call-update
  8.6 0.0 all-gather.10.cloned.1.call-start
  8.7 0.7 all-gather.10.cloned.1.call-update
  9.4 0.0 all-gather.12.cloned.1.call-start
  9.4 0.5 all-gather.12.cloned.1.call-update
  10.0 0.0 all-gather.14.cloned.1.call-start
  10.0 49.5 %all_gather.22 = bf16[256,512]{1,0:T(8,128)(2,1)} all-gather(bf16[8,512]{1,0:T(8,128)(2,1)} %param.11), channel_id=1, replica_groups=mesh['var'=32,'tp'=8] {'var'}, dimensions={0}, use_global_device_ids=true | all-gather | bytes 270336 | tf_op jit(solution)/shard_map/all_gather | solution.py:22
  59.5 0.0 all-gather.14.cloned.1.call-update
  59.5 0.0 all-reduce.2.cloned.1.call-start
  60.2 0.7 reduce
  60.9 13.4 %all-gather.6.cloned.1.call-done = bf16[4096,256]{1,0:T(8,128)(2,1)} async-done(((bf16[128,256]{1,0:T(8,128)(2,1)}), bf16[4096,256]{1,0:T(8,128)(2,1)}) %all-gather.6.cloned.1.call-update) | async-done | bytes 2097168 | tf_op jit(solution)/shard_map/all_gather | solution.py:11
  74.4 0.0 copy-start
  74.4 69.0 %all-gather.8.cloned.1.call-done = bf16[4096,896]{1,0:T(8,128)(2,1)} async-done(((bf16[128,896]{1,0:T(8,128)(2,1)}), bf16[4096,896]{1,0:T(8,128)(2,1)}) %all-gather.8.cloned.1.call-update) | async-done | bytes 7340048 | tf_op jit(solution)/shard_map/all_gather | solution.py:12
  143.3 7.0 %fusion.5 = f32[256,896]{1,0:T(8,128)} fusion(bf16[4096,256]{1,0:T(8,128)(2,1)} %all-gather.6.cloned.1.call-done, bf16[4096,896]{1,0:T(8,128)(2,1)} %all-gather.8.cloned.1.call-done), kind=kOutput, calls=%fused_computation.12 | convolution fusion | flops 1879048192 | bytes 10354688 | tf_op jit(solution)/shard_map/dot_general | solution.py:14
  150.3 61.7 %all-gather.10.cloned.1.call-done = bf16[4096,896]{1,0:T(8,128)(2,1)} async-done(((bf16[128,896]{1,0:T(8,128)(2,1)}), bf16[4096,896]{1,0:T(8,128)(2,1)}) %all-gather.10.cloned.1.call-update) | async-done | bytes 7340048 | tf_op jit(solution)/shard_map/all_gather | solution.py:13
  212.1 0.0 copy-done
  212.1 5.7 convolution_multiply_fusion.1
  217.7 77.8 %all-gather.12.cloned.1.call-done = bf16[896,4096]{1,0:T(8,128)(2,1)} async-done(((bf16[896,128]{1,0:T(8,128)(2,1)}), bf16[896,4096]{1,0:T(8,128)(2,1)}) %all-gather.12.cloned.1.call-update) | async-done | bytes 7340048 | tf_op jit(solution)/shard_map/all_gather | solution.py:20
  295.5 7.4 %fusion.2 = f32[256,4096]{1,0:T(8,128)} fusion(bf16[896,4096]{1,0:T(8,128)(2,1)} %all-gather.12.cloned.1.call-done, f32[256,896]{1,0:T(8,128)S(1)} %convolution_multiply_fusion.1, f32[896]{0:T(1024)S(1)} %fusion.3, f32[896]{0:T(1024)S(1)} %reduce), kind=kOutput, calls=%fused_computation.7 | convolution fusion | flops 1879736320 | bytes 12459008 | tf_op jit(solution)/shard_map/dot_general | solution.py:21
  303.0 0.0 all-reduce.2.cloned.1.call-update
  303.0 68.9 %all-gather.14.cloned.1.call-done = bf16[256,4096]{1,0:T(8,128)(2,1)} async-done(((bf16[256,512]{1,0:T(8,128)(2,1)}), bf16[256,4096]{1,0:T(8,128)(2,1)}) %all-gather.14.cloned.1.call-update) | async-done | bytes 2097168 | tf_op jit(solution)/shard_map/all_gather | solution.py:24
  371.9 0.0 copy-start.2
  371.9 197.8 %all-reduce.2.cloned.1.call-done = f32[256,4096]{1,0:T(8,128)} async-done(((f32[256,4096]{1,0:T(8,128)}), f32[256,4096]{1,0:T(8,128)}) %all-reduce.2.cloned.1.call-update) | async-done | bytes 4194320 | tf_op jit(solution)/shard_map/psum | solution.py:23
  569.7 0.0 copy-start.1
  569.7 7.4 %fusion.1 = f32[896]{0:T(1024)S(1)} fusion(f32[256,896]{1,0:T(8,128)S(1)} %convolution_multiply_fusion.1, bf16[896,4096]{1,0:T(8,128)(2,1)} %all-gather.12.cloned.1.call-done, f32[256,4096]{1,0:T(8,128)} %all-reduce.2.cloned.1.call-done, bf16[256,4096]{1,0:T(8,128)(2,1)} %all-gather.14.cloned.1.call-done), kind=kOutput, calls=%fused_computation.5 | convolution fusion | flops 1882651776 | bytes 14552576 | tf_op jit(solution)/shard_map/dot_general | solution.py:29
  577.1 0.6 fusion.4
  577.7 0.0 copy-done.2
  577.7 0.0 copy-done.1
  577.7 5.2 fusion
  (1 shorter events, 0.0 us)
Async XLA Ops:
  7.2 67.2 %all-gather.6.cloned.1.call-start = ((), (), s32[]{:S(2)}) async-start(), calls=%async_computation | async-start | bytes 2162688 | tf_op jit(solution)/shard_map/all_gather | solution.py:11
  7.9 135.4 %all-gather.8.cloned.1.call-start = ((), (), s32[]{:S(2)}) async-start(), calls=%async_computation.1 | async-start | bytes 7569408 | tf_op jit(solution)/shard_map/all_gather | solution.py:12
  8.6 203.4 %all-gather.10.cloned.1.call-start = ((), (), s32[]{:S(2)}) async-start(), calls=%async_computation.2 | async-start | bytes 7569408 | tf_op jit(solution)/shard_map/all_gather | solution.py:13
  9.4 286.1 %all-gather.12.cloned.1.call-start = ((), (), s32[]{:S(2)}) async-start(), calls=%async_computation.3 | async-start | bytes 7569408 | tf_op jit(solution)/shard_map/all_gather | solution.py:20
  10.0 361.9 %all-gather.14.cloned.1.call-start = ((), (), s32[]{:S(2)}) async-start(), calls=%async_computation.5 | async-start | bytes 2359296 | tf_op jit(solution)/shard_map/all_gather | solution.py:24
  59.5 510.2 %all-reduce.2.cloned.1.call-start = ((), (), s32[]{:S(2)}) async-start(), calls=%async_computation.4 | async-start | bytes 8388608 | tf_op jit(solution)/shard_map/psum | solution.py:23
  74.4 137.7 %copy-start = (bf16[4096,256]{1,0:T(8,128)(2,1)S(1)}, bf16[4096,256]{1,0:T(8,128)(2,1)}, u32[]{:S(2)}) copy-start(bf16[4096,256]{1,0:T(8,128)(2,1)} %all-gather.6.cloned.1.call-done) | copy-start | bytes 6291460
  371.9 205.8 %copy-start.2 = (bf16[256,4096]{1,0:T(8,128)(2,1)S(1)}, bf16[256,4096]{1,0:T(8,128)(2,1)}, u32[]{:S(2)}) copy-start(bf16[256,4096]{1,0:T(8,128)(2,1)} %all-gather.14.cloned.1.call-done) | copy-start | bytes 6291460
  569.7 8.1 %copy-start.1 = (f32[256,4096]{1,0:T(8,128)S(1)}, f32[256,4096]{1,0:T(8,128)}, u32[]{:S(2)}) copy-start(f32[256,4096]{1,0:T(8,128)} %all-reduce.2.cloned.1.call-done) | copy-start | bytes 12582916
Sparse Core Ops, SparseCore 0:
  9.9 64.4 all-gather.5
  76.2 67.0 all-gather.7
  145.2 66.8 all-gather.9
  213.7 81.7 all-gather.11
  297.8 74.0 all-gather.13
  375.0 194.6 all-reduce.1
where the time goes:
time: 590 us
  waiting for transfers between devices  491 us (83%)
  blocking collectives  49.5 us (8%)
  matrix products  32.8 us (6%)
  between operations  14.8 us (3%)
    psum x1, waiting for transfers between devices, local(): output = lax.psum(partial_value, 'tp')  198 us
    all_gather x1, waiting for transfers between devices, local(): down_whole = lax.all_gather(down_parent, 'var', axis=1, tiled=True)  77.8 us
    all_gather x1, waiting for transfers between devices, local(): gate_piece = lax.all_gather(gate_parent, 'var', axis=0, tiled=True)  69 us
    all_gather x1, waiting for transfers between devices, local(): target_whole = lax.all_gather(target_part, 'tp', axis=1, tiled=True)  68.9 us
    all_gather x1, waiting for transfers between devices, local(): up_piece = lax.all_gather(up_parent, 'var', axis=0, tiled=True)  61.7 us
    all_gather x1, blocking collectives, local(): target_part = lax.all_gather(targets, 'var', axis=0, tiled=True)  49.5 us
    all_gather x1, waiting for transfers between devices, local(): feats = lax.all_gather(parent_inputs, 'var', axis=0, tiled=True)  13.4 us
  transfers between devices with their start and end apart: 6, of which 6 were waited for; matrix products, arithmetic and copies ran while one was open for 4% of the time, Pallas kernels for 0%

commit v1 on v0

--- a/solution.py
+++ b/solution.py
@@ -8,7 +8,10 @@
     contract_rows = (((0,), (0,)), ((), ()))
     rows = parent_inputs.shape[1]
     local_ff = gate_parent.shape[1]
-    feats = lax.all_gather(parent_inputs, "var", axis=0, tiled=True)
+    peers = lax.axis_size("var")
+    blocks = jnp.stack([parent_inputs for _ in range(peers)])
+    blocks = lax.all_to_all(blocks, "var", split_axis=0, concat_axis=0)
+    feats = jnp.concatenate(blocks, axis=0)
     gate_piece = lax.all_gather(gate_parent, "var", axis=0, tiled=True)
     up_piece = lax.all_gather(up_parent, "var", axis=0, tiled=True)
     gate_sum = lax.dot_general(feats, gate_piece, contract_rows, preferred_element_type=jnp.float32)

time: 590 us -> 562 us (0.953)
  waiting for transfers between devices: 491 us -> 411 us
  blocking collectives: 49.5 us -> 90.4 us
  starting transfers between devices: 0.23 us -> 10.2 us
    all_gather x1, waiting for transfers between devices: 69 us -> 1.92 us  [local(): gate_piece = lax.all_gather(gate_parent, 'var', axis=0, tiled=True)]
    all_gather x1, blocking collectives: 49.5 us -> 90.4 us  [local(): target_part = lax.all_gather(targets, 'var', axis=0, tiled=True)]
    all_gather x1 -> x0, waiting for transfers between devices: 13.4 us -> none  [local(): feats = lax.all_gather(parent_inputs, 'var', axis=0, tiled=True)]
    all_to_all x0 -> x1, starting transfers between devices: none -> 10 us  [local(): blocks = lax.all_to_all(blocks, 'var', split_axis=0, concat_axis=0)]
  transfers between devices with their start and end apart: 6 -> 6, of which waited for: 6 -> 5; matrix products, arithmetic and copies ran while one was open for 4% -> 4% of each run, Pallas kernels for 0% -> 0%
where the time goes in v1:
time: 562 us
  waiting for transfers between devices  411 us (73%)
  blocking collectives  90.4 us (16%)
  matrix products  32.1 us (6%)
  between operations  14.5 us (3%)
  starting transfers between devices  10.2 us (2%)
    psum x1, waiting for transfers between devices, local(): output = lax.psum(partial_value, 'tp')  198 us
    all_gather x1, blocking collectives, local(): target_part = lax.all_gather(targets, 'var', axis=0, tiled=True)  90.4 us
    all_gather x1, waiting for transfers between devices, local(): down_whole = lax.all_gather(down_parent, 'var', axis=1, tiled=True)  77.9 us
    all_gather x1, waiting for transfers between devices, local(): target_whole = lax.all_gather(target_part, 'tp', axis=1, tiled=True)  68.9 us
    all_gather x1, waiting for transfers between devices, local(): up_piece = lax.all_gather(up_parent, 'var', axis=0, tiled=True)  62.8 us
  transfers between devices with their start and end apart: 6, of which 5 were waited for; matrix products, arithmetic and copies ran while one was open for 4% of the time, Pallas kernels for 0%

profile of v1, /device:TPU:1, one launch (start us, length us, event | category | flops | bytes accessed | tf_op | source)
XLA Modules:
  0.0 561.7 jit_solution(8641350675801830565)
XLA Ops:
  7.2 0.0 copy-start.2
  7.2 0.0 copy-start.3
  7.2 0.0 all-gather.5.cloned.1.call-start
  7.2 0.7 all-gather.5.cloned.1.call-update
  7.9 0.0 all-gather.7.cloned.1.call-start
  8.0 0.7 all-gather.7.cloned.1.call-update
  8.7 0.0 all-gather.9.cloned.1.call-start
  8.7 0.7 all-gather.9.cloned.1.call-update
  9.4 2.4 stack.2
  11.8 10.0 %all-to-all-start = ((bf16[32,128,256]{2,1,0:T(8,128)(2,1)}), bf16[32,128,256]{2,1,0:T(8,128)(2,1)S(1)}, u32[]{:S(2)}, u32[]{:S(2)}) async-start(bf16[32,128,256]{2,1,0:T(8,128)(2,1)} %stack.2), calls=%async_computation | async-start | bytes 4194304 | tf_op jit(solution)/shard_map/all_to_all | solution.py:13
  21.8 0.0 all-gather.11.cloned.1.call-start
  21.9 0.0 copy-done.2
  21.9 90.4 %all_gather.18 = bf16[256,512]{1,0:T(8,128)(2,1)} all-gather(bf16[8,512]{1,0:T(8,128)(2,1)S(1)} %copy-done.2), channel_id=1, replica_groups=mesh['var'=32,'tp'=8] {'var'}, dimensions={0}, use_global_device_ids=true | all-gather | bytes 270336 | tf_op jit(solution)/shard_map/all_gather | solution.py:25
  112.3 0.0 all-gather.11.cloned.1.call-update
  112.3 0.0 all-reduce.2.cloned.1.call-start
  113.0 0.0 copy-done.3
  113.0 0.0 all-to-all-done
  113.0 1.9 all-gather.5.cloned.1.call-done
  115.0 6.4 %fusion.5 = f32[256,896]{1,0:T(8,128)} fusion(bf16[4096,256]{1,0:T(8,128)(2,1)S(1)} %bitcast.12, bf16[4096,896]{1,0:T(8,128)(2,1)} %all-gather.5.cloned.1.call-done), kind=kOutput, calls=%fused_computation.12 | convolution fusion | flops 1879048192 | bytes 10354688 | tf_op jit(solution)/shard_map/dot_general | solution.py:17
  121.3 62.8 %all-gather.7.cloned.1.call-done = bf16[4096,896]{1,0:T(8,128)(2,1)} async-done(((bf16[128,896]{1,0:T(8,128)(2,1)}), bf16[4096,896]{1,0:T(8,128)(2,1)}) %all-gather.7.cloned.1.call-update) | async-done | bytes 7340048 | tf_op jit(solution)/shard_map/all_gather | solution.py:16
  184.1 5.7 %convolution_multiply_fusion.1 = f32[256,896]{1,0:T(8,128)S(1)} fusion(bf16[4096,256]{1,0:T(8,128)(2,1)S(1)} %bitcast.13, bf16[4096,896]{1,0:T(8,128)(2,1)} %all-gather.7.cloned.1.call-done, f32[256,896]{1,0:T(8,128)} %fusion.5), kind=kOutput, calls=%fused_computation.4 | convolution fusion | flops 1880195072 | bytes 11272192 | tf_op jit(solution)/shard_map/dot_general | solution.py:18
  189.8 77.9 %all-gather.9.cloned.1.call-done = bf16[896,4096]{1,0:T(8,128)(2,1)} async-done(((bf16[896,128]{1,0:T(8,128)(2,1)}), bf16[896,4096]{1,0:T(8,128)(2,1)}) %all-gather.9.cloned.1.call-update) | async-done | bytes 7340048 | tf_op jit(solution)/shard_map/all_gather | solution.py:23
  267.7 7.4 %fusion.2 = f32[256,4096]{1,0:T(8,128)} fusion(bf16[896,4096]{1,0:T(8,128)(2,1)} %all-gather.9.cloned.1.call-done, f32[256,896]{1,0:T(8,128)S(1)} %convolution_multiply_fusion.1, f32[896]{0:T(1024)S(1)} %fusion.3, f32[896]{0:T(1024)S(1)} %reduce), kind=kOutput, calls=%fused_computation.7 | convolution fusion | flops 1879736320 | bytes 12459008 | tf_op jit(solution)/shard_map/dot_general | solution.py:24
  275.2 0.0 all-reduce.2.cloned.1.call-update
  275.2 68.9 %all-gather.11.cloned.1.call-done = bf16[256,4096]{1,0:T(8,128)(2,1)} async-done(((bf16[256,512]{1,0:T(8,128)(2,1)}), bf16[256,4096]{1,0:T(8,128)(2,1)}) %all-gather.11.cloned.1.call-update) | async-done | bytes 2097168 | tf_op jit(solution)/shard_map/all_gather | solution.py:27
  344.1 0.0 copy-start.1
  344.1 197.7 %all-reduce.2.cloned.1.call-done = f32[256,4096]{1,0:T(8,128)} async-done(((f32[256,4096]{1,0:T(8,128)}), f32[256,4096]{1,0:T(8,128)}) %all-reduce.2.cloned.1.call-update) | async-done | bytes 4194320 | tf_op jit(solution)/shard_map/psum | solution.py:26
  541.9 0.0 copy-start
  541.9 7.4 %fusion.1 = f32[896]{0:T(1024)S(1)} fusion(f32[256,896]{1,0:T(8,128)S(1)} %convolution_multiply_fusion.1, bf16[896,4096]{1,0:T(8,128)(2,1)} %all-gather.9.cloned.1.call-done, f32[256,4096]{1,0:T(8,128)} %all-reduce.2.cloned.1.call-done, bf16[256,4096]{1,0:T(8,128)(2,1)} %all-gather.11.cloned.1.call-done), kind=kOutput, calls=%fused_computation.5 | convolution fusion | flops 1882651776 | bytes 14552576 | tf_op jit(solution)/shard_map/dot_general | solution.py:32
  549.3 0.6 fusion.4
  549.9 0.0 copy-done.1
  549.9 0.0 copy-done
  549.9 5.2 fusion
  (2 shorter events, 0.0 us)
Async XLA Ops:
  7.2 14.7 %copy-start.2 = (bf16[8,512]{1,0:T(8,128)(2,1)S(1)}, bf16[8,512]{1,0:T(8,128)(2,1)}, u32[]{:S(2)}) copy-start(bf16[8,512]{1,0:T(8,128)(2,1)} %param.11) | copy-start | bytes 24580
  7.2 105.8 %copy-start.3 = (f32[1,896]{1,0:T(1,128)S(1)}, f32[1,896]{1,0:T(1,128)}, u32[]{:S(2)}) copy-start(f32[1,896]{1,0:T(1,128)} %param.13) | copy-start | bytes 10756
  7.2 107.8 %all-gather.5.cloned.1.call-start = ((), (), s32[]{:S(2)}) async-start(), calls=%async_computation.1 | async-start | bytes 7569408 | tf_op jit(solution)/shard_map/all_gather | solution.py:15
  7.9 176.2 %all-gather.7.cloned.1.call-start = ((), (), s32[]{:S(2)}) async-start(), calls=%async_computation.2 | async-start | bytes 7569408 | tf_op jit(solution)/shard_map/all_gather | solution.py:16
  8.7 259.0 %all-gather.9.cloned.1.call-start = ((), (), s32[]{:S(2)}) async-start(), calls=%async_computation.3 | async-start | bytes 7569408 | tf_op jit(solution)/shard_map/all_gather | solution.py:23
  11.8 101.2 %all-to-all-start = ((bf16[32,128,256]{2,1,0:T(8,128)(2,1)}), bf16[32,128,256]{2,1,0:T(8,128)(2,1)S(1)}, u32[]{:S(2)}, u32[]{:S(2)}) async-start(bf16[32,128,256]{2,1,0:T(8,128)(2,1)} %stack.2), calls=%async_computation | async-start | bytes 4194304 | tf_op jit(solution)/shard_map/all_to_all | solution.py:13
  21.8 322.3 %all-gather.11.cloned.1.call-start = ((), (), s32[]{:S(2)}) async-start(), calls=%async_computation.5 | async-start | bytes 2359296 | tf_op jit(solution)/shard_map/all_gather | solution.py:27
  112.3 429.6 %all-reduce.2.cloned.1.call-start = ((), (), s32[]{:S(2)}) async-start(), calls=%async_computation.4 | async-start | bytes 8388608 | tf_op jit(solution)/shard_map/psum | solution.py:26
  344.1 205.8 %copy-start.1 = (bf16[256,4096]{1,0:T(8,128)(2,1)S(1)}, bf16[256,4096]{1,0:T(8,128)(2,1)}, u32[]{:S(2)}) copy-start(bf16[256,4096]{1,0:T(8,128)(2,1)} %all-gather.11.cloned.1.call-done) | copy-start | bytes 6291460
  541.9 8.0 %copy-start = (f32[256,4096]{1,0:T(8,128)S(1)}, f32[256,4096]{1,0:T(8,128)}, u32[]{:S(2)}) copy-start(f32[256,4096]{1,0:T(8,128)} %all-reduce.2.cloned.1.call-done) | copy-start | bytes 12582916
Sparse Core Ops, SparseCore 0:
  9.9 105.0 all-gather.4
  116.8 67.2 all-gather.6
  185.9 81.7 all-gather.8
  270.0 74.0 all-gather.10
  347.2 194.6 all-reduce.1
